TPU v7x, 512 devices: a whole 4x8x8 slice. The times are simulated.
512 devices in a mesh: grp: 16 (over x, z_hi), body: 32 (over y, z_lo, core).
Axes of the slice: x: 4, y: 8, z: 8 (z_hi: 4, z_lo: 2; z = z_hi * 2 + z_lo), core: 2. Of those that a mesh axis runs over, the one named last changes fastest.
Arguments:
- incident: bfloat16 [512, 16, 512], P(('grp', 'body')), may hold values from -6 to 6
- exciting: float32 [512, 16, 512], P(('grp', 'body')), may hold values from -6 to 6
- t_matrices: bfloat16 [512, 2, 256, 256], P(('grp', 'body')), may hold values from -0.1875 to 0.1875
- hankel_rows: bfloat16 [225, 2, 512], replicated, may hold values from -0.046875 to 0.046875
- offsets: int32 [512, 32], P(('grp', 'body')), may hold values from 0 to 224
- lattice_slots: int32 [512], P('grp'), may hold values from 0 to 31, as said below
- up_maps: bfloat16 [512, 2, 256, 512], P(('grp', 'body')), may hold values from -0.0625 to 0.0625
- down_maps: bfloat16 [512, 2, 512, 256], P(('grp', 'body')), may hold values from -0.1875 to 0.1875
- group_maps: bfloat16 [16, 16, 2, 512, 512], P('grp', None, None, 'body'), may hold values from -0.046875 to 0.046875
Outputs:
- updated: float32 [512, 16, 512], P(('grp', 'body'))
Inputs may be any that keep to these rules, and one draw needn't show every extreme that they name: `lattice_slots`: within each group the 32 columns stand at the slots 0 to 31, one column a slot.
All inputs are finite; a program needn't handle non-finite values.
Results may differ from a plain program's by a relative error of at most 0.0034.
Values may be sent and summed in bfloat16 or wider, within the bound.
A program may use at most 64 MiB of HBM per device.

v0:
```python
import math
import jax
import jax.numpy as jnp
from jax import lax
from jax.sharding import PartitionSpec as P


def complex_apply(form, values, real_mats, imag_mats):
    half_width = values.shape[-1] // 2
    real_values = values[..., :half_width]
    imag_values = values[..., half_width:]
    real_out = jnp.einsum(
        form, real_values, real_mats, preferred_element_type=jnp.float32
    ) - jnp.einsum(form, imag_values, imag_mats, preferred_element_type=jnp.float32)
    imag_out = jnp.einsum(
        form, real_values, imag_mats, preferred_element_type=jnp.float32
    ) + jnp.einsum(form, imag_values, real_mats, preferred_element_type=jnp.float32)
    return jnp.concatenate([real_out, imag_out], axis=-1)


def toeplitz_mats(sequences):
    length = sequences.shape[-1] // 2
    repeats = (1,) * (sequences.ndim - 1) + (length,)
    tiled = jnp.tile(sequences, repeats)
    window = tiled[..., length : length + length * (2 * length - 1)]
    return window.reshape(sequences.shape[:-1] + (length, 2 * length - 1))[..., :length]


def local(
    incident,
    exciting,
    t_matrices,
    hankel_rows,
    offsets,
    lattice_slots,
    up_maps,
    down_maps,
    group_maps,
):
    body_index = lax.axis_index("body")
    group_index = lax.axis_index("grp")
    local_count = incident.shape[0]
    scattered = complex_apply("iln,inm->ilm", incident, t_matrices[:, 0], t_matrices[:, 1]).astype(
        jnp.bfloat16
    )
    own_members = body_index * local_count + jnp.arange(local_count, dtype=jnp.int32)
    zero_seq = jnp.zeros((), jnp.bfloat16)
    all_offsets = lax.all_gather(offsets, "body", axis=0, tiled=True)
    group_count = lattice_slots.shape[0]
    own_slots = lax.dynamic_slice_in_dim(lattice_slots, body_index * local_count, local_count, 0)
    table_rows = jnp.take(all_offsets, own_slots, axis=1)
    sequences = jnp.take(hankel_rows, table_rows, axis=0)
    targets = jnp.arange(group_count, dtype=jnp.int32)
    keep = targets[:, None] != own_members[None, :]
    sequences = jnp.where(keep[:, :, None, None], sequences, zero_seq)
    block_rows = math.gcd(group_count, 4)
    sequences = sequences.reshape((group_count // block_rows, block_rows) + sequences.shape[1:])

    def one_block(block_seqs):
        mats = toeplitz_mats(block_seqs)
        return complex_apply("sln,tsnm->tlm", scattered, mats[:, :, 0], mats[:, :, 1])

    terms = lax.map(one_block, sequences)
    totals = lax.psum(terms.reshape((group_count,) + terms.shape[2:]), "body")
    near = lax.dynamic_slice_in_dim(totals, body_index * local_count, local_count, 0)
    partial_value = complex_apply("iln,inq->lq", scattered, up_maps[:, 0], up_maps[:, 1])
    expansion = lax.psum(partial_value, "body").astype(jnp.bfloat16)
    block_width = group_maps.shape[3]
    full_width = group_maps.shape[4]
    real_block = lax.dynamic_slice_in_dim(expansion, body_index * block_width, block_width, 1)
    imag_block = lax.dynamic_slice_in_dim(
        expansion, full_width + body_index * block_width, block_width, 1
    )
    own_block = jnp.concatenate([real_block, imag_block], axis=-1)[None]
    piece = lax.all_gather(own_block, "grp", axis=0, tiled=True)
    width = piece.shape[0]
    sources = jnp.arange(width, dtype=jnp.int32)
    piece = jnp.where((sources != group_index)[:, None, None], piece, zero_seq)
    mats = group_maps[0]
    incoming_part = complex_apply("hln,hnq->lq", piece, mats[:, 0], mats[:, 1])
    incoming = lax.psum(incoming_part, "body").astype(jnp.bfloat16)
    far = complex_apply("lq,iqp->ilp", incoming, down_maps[:, 0], down_maps[:, 1])
    return exciting + near + far


def solution(mesh):
    return jax.shard_map(
        local,
        mesh=mesh,
        in_specs=(
            P(("grp", "body"), None, None),
            P(("grp", "body"), None, None),
            P(("grp", "body"), None, None, None),
            P(),
            P(("grp", "body"), None),
            P("grp"),
            P(("grp", "body"), None, None, None),
            P(("grp", "body"), None, None, None),
            P("grp", None, None, "body", None),
        ),
        out_specs=P(("grp", "body"), None, None),
        check_vma=False,
    )
```

profile of v0, /device:TPU:32, one launch (start us, length us, event | category | flops | bytes accessed | tf_op | source)
XLA Modules:
  0.0 437.4 jit_solution(12570242964982283185)
XLA Ops:
  12.1 32.7 %all-gather.1 = s32[32,1,32]{2,1,0:T(1,128)S(1)} all-gather(s32[1,1,32]{2,1,0:T(1,128)} %bitcast.159), channel_id=1, replica_groups=mesh['grp'=16,'body'=32] {'body'}, dimensions={0}, use_global_device_ids=true | all-gather | bytes 4224 | tf_op jit(solution)/shard_map/all_gather | solution.py:48
  49.3 119.1 %while.11 = (s32[]{:T(128)}, f32[8,4,16,512]{3,2,1,0:T(8,128)}, bf16[8,4,1,2,512]{4,3,1,2,0:T(2,128)(2,1)S(1)}, bf16[1,16,512]{2,1,0:T(8,128)(2,1)S(1)}, s32[]{:T(128)}) while((s32[]{:T(128)}, f32[8,4,16,512]{3,2,1,0:T(8,128)}, bf16[8,4,1,2,512]{4,3,1,2,0:T(2,128)(2,1)S(1)}, bf16[1,16,512]{2,1,0:T(8,128)(2,1)S(1)}, s32[]{:T(128)}) %tuple.28), condition=%wide.region_1.2_spmd, body=%wide.region_0.1_spmd.sunk | while | flops 33619968 | bytes 17474112 | solution.py:63
  49.5 2.8 tile.14
  52.3 4.4 %slice.219 = bf16[4,1,2,130816]{3,2,0,1:T(2,128)(2,1)} slice(bf16[4,1,2,131072]{3,2,0,1:T(2,128)(2,1)} %tile.14), slice={[0:4], [0:1], [0:2], [256:131072]} | slice | bytes 4186112 | tf_op jit(solution)/shard_map/while/body/eval_jaxpr/slice | solution.py:25
  56.7 6.1 %reshape.288 = bf16[4,1,2,256,511]{4,3,2,0,1:T(8,128)(2,1)S(1)} reshape(bf16[4,1,2,130816]{3,2,0,1:T(2,128)(2,1)} %slice.219) | data formatting | bytes 4186112 | tf_op jit(solution)/shard_map/while/body/eval_jaxpr/reshape | solution.py:26
  64.4 2.8 tile.14
  67.2 4.4 %slice.219 = bf16[4,1,2,130816]{3,2,0,1:T(2,128)(2,1)} slice(bf16[4,1,2,131072]{3,2,0,1:T(2,128)(2,1)} %tile.14), slice={[0:4], [0:1], [0:2], [256:131072]} | slice | bytes 4186112 | tf_op jit(solution)/shard_map/while/body/eval_jaxpr/slice | solution.py:25
  71.6 6.1 %reshape.288 = bf16[4,1,2,256,511]{4,3,2,0,1:T(8,128)(2,1)S(1)} reshape(bf16[4,1,2,130816]{3,2,0,1:T(2,128)(2,1)} %slice.219) | data formatting | bytes 4186112 | tf_op jit(solution)/shard_map/while/body/eval_jaxpr/reshape | solution.py:26
  79.2 2.8 tile.14
  82.0 4.4 %slice.219 = bf16[4,1,2,130816]{3,2,0,1:T(2,128)(2,1)} slice(bf16[4,1,2,131072]{3,2,0,1:T(2,128)(2,1)} %tile.14), slice={[0:4], [0:1], [0:2], [256:131072]} | slice | bytes 4186112 | tf_op jit(solution)/shard_map/while/body/eval_jaxpr/slice | solution.py:25
  86.4 6.1 %reshape.288 = bf16[4,1,2,256,511]{4,3,2,0,1:T(8,128)(2,1)S(1)} reshape(bf16[4,1,2,130816]{3,2,0,1:T(2,128)(2,1)} %slice.219) | data formatting | bytes 4186112 | tf_op jit(solution)/shard_map/while/body/eval_jaxpr/reshape | solution.py:26
  96.9 4.4 %slice.219 = bf16[4,1,2,130816]{3,2,0,1:T(2,128)(2,1)} slice(bf16[4,1,2,131072]{3,2,0,1:T(2,128)(2,1)} %tile.14), slice={[0:4], [0:1], [0:2], [256:131072]} | slice | bytes 4186112 | tf_op jit(solution)/shard_map/while/body/eval_jaxpr/slice | solution.py:25
  101.3 6.1 %reshape.288 = bf16[4,1,2,256,511]{4,3,2,0,1:T(8,128)(2,1)S(1)} reshape(bf16[4,1,2,130816]{3,2,0,1:T(2,128)(2,1)} %slice.219) | data formatting | bytes 4186112 | tf_op jit(solution)/shard_map/while/body/eval_jaxpr/reshape | solution.py:26
  111.8 4.4 %slice.219 = bf16[4,1,2,130816]{3,2,0,1:T(2,128)(2,1)} slice(bf16[4,1,2,131072]{3,2,0,1:T(2,128)(2,1)} %tile.14), slice={[0:4], [0:1], [0:2], [256:131072]} | slice | bytes 4186112 | tf_op jit(solution)/shard_map/while/body/eval_jaxpr/slice | solution.py:25
  116.2 6.1 %reshape.288 = bf16[4,1,2,256,511]{4,3,2,0,1:T(8,128)(2,1)S(1)} reshape(bf16[4,1,2,130816]{3,2,0,1:T(2,128)(2,1)} %slice.219) | data formatting | bytes 4186112 | tf_op jit(solution)/shard_map/while/body/eval_jaxpr/reshape | solution.py:26
  126.7 4.4 %slice.219 = bf16[4,1,2,130816]{3,2,0,1:T(2,128)(2,1)} slice(bf16[4,1,2,131072]{3,2,0,1:T(2,128)(2,1)} %tile.14), slice={[0:4], [0:1], [0:2], [256:131072]} | slice | bytes 4186112 | tf_op jit(solution)/shard_map/while/body/eval_jaxpr/slice | solution.py:25
  131.1 6.1 %reshape.288 = bf16[4,1,2,256,511]{4,3,2,0,1:T(8,128)(2,1)S(1)} reshape(bf16[4,1,2,130816]{3,2,0,1:T(2,128)(2,1)} %slice.219) | data formatting | bytes 4186112 | tf_op jit(solution)/shard_map/while/body/eval_jaxpr/reshape | solution.py:26
  141.6 4.4 %slice.219 = bf16[4,1,2,130816]{3,2,0,1:T(2,128)(2,1)} slice(bf16[4,1,2,131072]{3,2,0,1:T(2,128)(2,1)} %tile.14), slice={[0:4], [0:1], [0:2], [256:131072]} | slice | bytes 4186112 | tf_op jit(solution)/shard_map/while/body/eval_jaxpr/slice | solution.py:25
  146.0 6.1 %reshape.288 = bf16[4,1,2,256,511]{4,3,2,0,1:T(8,128)(2,1)S(1)} reshape(bf16[4,1,2,130816]{3,2,0,1:T(2,128)(2,1)} %slice.219) | data formatting | bytes 4186112 | tf_op jit(solution)/shard_map/while/body/eval_jaxpr/reshape | solution.py:26
  156.4 4.4 %slice.219 = bf16[4,1,2,130816]{3,2,0,1:T(2,128)(2,1)} slice(bf16[4,1,2,131072]{3,2,0,1:T(2,128)(2,1)} %tile.14), slice={[0:4], [0:1], [0:2], [256:131072]} | slice | bytes 4186112 | tf_op jit(solution)/shard_map/while/body/eval_jaxpr/slice | solution.py:25
  160.8 6.1 %reshape.288 = bf16[4,1,2,256,511]{4,3,2,0,1:T(8,128)(2,1)S(1)} reshape(bf16[4,1,2,130816]{3,2,0,1:T(2,128)(2,1)} %slice.219) | data formatting | bytes 4186112 | tf_op jit(solution)/shard_map/while/body/eval_jaxpr/reshape | solution.py:26
  169.0 104.8 %psum.22 = bf16[16,1024]{1,0:T(8,128)(2,1)S(1)} all-reduce(f32[16,1024]{1,0:T(8,128)S(1)} %pad_maximum_fusion), channel_id=1, replica_groups=mesh['grp'=16,'body'=32] {'body'}, use_global_device_ids=true, to_apply=%region_3.4 | all-reduce | flops 16384 | bytes 98304 | tf_op jit(solution)/shard_map/psum | solution.py:67
  274.0 48.7 %all-gather = bf16[256,32]{1,0:T(8,128)(2,1)S(1)} all-gather(bf16[16,32]{1,0:T(8,128)(2,1)S(1)} %pad_maximum_fusion.3), channel_id=2, replica_groups=mesh['grp'=16,'body'=32] {'grp'}, dimensions={0}, use_global_device_ids=true | all-gather | bytes 17408 | tf_op jit(solution)/shard_map/all_gather | solution.py:75
  324.0 104.5 %psum.23 = bf16[16,1024]{1,0:T(8,128)(2,1)S(1)} all-reduce(f32[16,1024]{1,0:T(8,128)S(1)} %pad_maximum_fusion.1), channel_id=1, replica_groups=mesh['grp'=16,'body'=32] {'body'}, use_global_device_ids=true, to_apply=%region_4.5 | all-reduce | flops 16384 | bytes 98304 | tf_op jit(solution)/shard_map/psum | solution.py:81
  (107 shorter events, 38.6 us)
Async XLA Ops:
  6.5 41.9 %copy-start = (bf16[225,2,512]{2,1,0:T(2,128)(2,1)S(1)}, bf16[225,2,512]{2,1,0:T(2,128)(2,1)}, u32[]{:S(2)}) copy-start(bf16[225,2,512]{2,1,0:T(2,128)(2,1)} %param.14) | copy-start | bytes 1382404
  6.5 422.6 %all-reduce.2.cloned.1.call-start = ((), (), s32[]{:S(2)}) async-start(), calls=%async_computation | async-start | bytes 2097152 | tf_op jit(solution)/shard_map/psum | solution.py:64
  49.3 119.1 %copy-start.2 = (bf16[1,2,256,512]{3,2,1,0:T(8,128)(2,1)S(1)}, bf16[1,2,256,512]{3,2,1,0:T(8,128)(2,1)}, u32[]{:S(2)}) copy-start(bf16[1,2,256,512]{3,2,1,0:T(8,128)(2,1)} %param.17) | copy-start | bytes 1572868
  168.4 154.4 %copy-start.3 = (bf16[1,16,2,16,512]{4,3,2,1,0:T(8,128)(2,1)S(1)}, bf16[1,16,2,16,512]{4,3,2,1,0:T(8,128)(2,1)}, u32[]{:S(2)}) copy-start(bf16[1,16,2,16,512]{4,3,2,1,0:T(8,128)(2,1)} %param.19) | copy-start | bytes 1572868
  168.7 259.9 %copy-start.1 = (bf16[1,2,512,256]{3,2,1,0:T(8,128)(2,1)S(1)}, bf16[1,2,512,256]{3,2,1,0:T(8,128)(2,1)}, u32[]{:S(2)}) copy-start(bf16[1,2,512,256]{3,2,1,0:T(8,128)(2,1)} %param.18) | copy-start | bytes 1572868
  322.7 106.4 %copy-start.4 = (f32[1,16,512]{2,1,0:T(8,128)S(1)}, f32[1,16,512]{2,1,0:T(8,128)}, u32[]{:S(2)}) copy-start(f32[1,16,512]{2,1,0:T(8,128)} %param.12) | copy-start | bytes 98308
Sparse Core Ops, SparseCore 0:
  168.5 234.8 all-reduce.1
where the time goes:
time: 438 us; the launch traced here: 437 us
  blocking collectives  291 us (66%)
  local copies, waits for them, and re-layouts  110 us (25%)
  between operations  15.6 us (4%)
  matrix products  12.5 us (3%)
  other arithmetic  8.4 us (2%)
    psum x1, blocking collectives, local(): expansion = lax.psum(partial_value, 'body').astype(jnp.bfloat16)  105 us
    psum x1, blocking collectives, local(): incoming = lax.psum(incoming_part, 'body').astype(jnp.bfloat16)  105 us
    all_gather x1, blocking collectives, local(): piece = lax.all_gather(own_block, 'grp', axis=0, tiled=True)  48.7 us
    reshape x8, local copies, waits for them, and re-layouts, toeplitz_mats(): window.reshape(sequences.shape[:-1] + (length, 2 * length - 1))  48.7 us
    slice x8, local copies, waits for them, and re-layouts, toeplitz_mats(): window = tiled[..., length:length + length * (2 * length - 1)]  35.2 us
    all_gather x1, blocking collectives, local(): all_offsets = lax.all_gather(offsets, 'body', axis=0, tiled=True)  32.7 us
    another operation x24, local copies, waits for them, and re-layouts, toeplitz_mats(): tiled = jnp.tile(sequences, repeats)  23.8 us
  transfers between devices with their start and end apart: 1, of which 0 were waited for; matrix products, arithmetic and copies ran while one was open for 1% of the time, Pallas kernels for 0%

commit v1 on v0

--- a/solution.py
+++ b/solution.py
@@ -3,6 +3,12 @@
 import jax.numpy as jnp
 from jax import lax
 from jax.sharding import PartitionSpec as P
+
+
+def summed_here(block, name):
+    parts = lax.all_gather(block, name, axis=0, tiled=False)
+    result = parts.sum(axis=0)
+    return result
 
 
 def complex_apply(form, values, real_mats, imag_mats):
@@ -78,7 +84,7 @@
     piece = jnp.where((sources != group_index)[:, None, None], piece, zero_seq)
     mats = group_maps[0]
     incoming_part = complex_apply("hln,hnq->lq", piece, mats[:, 0], mats[:, 1])
-    incoming = lax.psum(incoming_part, "body").astype(jnp.bfloat16)
+    incoming = summed_here(incoming_part, "body").astype(jnp.bfloat16)
     far = complex_apply("lq,iqp->ilp", incoming, down_maps[:, 0], down_maps[:, 1])
     return exciting + near + far
 

time: 438 us -> 564 us (1.29)
  the two profiles are of different devices: /device:TPU:32 before, /device:TPU:1 now
where the time goes in v1:
time: 564 us; the launch traced here: 563 us
  waiting for transfers between devices  222 us (39%)
  blocking collectives  189 us (34%)
  local copies, waits for them, and re-layouts  109 us (19%)
  matrix products  16.4 us (3%)
  between operations  15.5 us (3%)
  other arithmetic  10.8 us (2%)
    psum x1, waiting for transfers between devices, local(): totals = lax.psum(terms.reshape((group_count,) + terms.shape[2:]), 'body')  222 us
    psum x1, blocking collectives, local(): expansion = lax.psum(partial_value, 'body').astype(jnp.bfloat16)  107 us
    reshape x8, local copies, waits for them, and re-layouts, toeplitz_mats(): window.reshape(sequences.shape[:-1] + (length, 2 * length - 1))  48.7 us
    all_gather x1, blocking collectives, local(): all_offsets = lax.all_gather(offsets, 'body', axis=0, tiled=True)  41.5 us
    all_gather x1, blocking collectives, local(): piece = lax.all_gather(own_block, 'grp', axis=0, tiled=True)  40.8 us
    slice x8, local copies, waits for them, and re-layouts, toeplitz_mats(): window = tiled[..., length:length + length * (2 * length - 1)]  35.1 us
    another operation x24, local copies, waits for them, and re-layouts, toeplitz_mats(): tiled = jnp.tile(sequences, repeats)  23.6 us
  transfers between devices with their start and end apart: 2, of which 1 were waited for; matrix products, arithmetic and copies ran while one was open for 22% of the time, Pallas kernels for 0%

profile of v1, /device:TPU:1, one launch (start us, length us, event | category | flops | bytes accessed | tf_op | source)
XLA Modules:
  0.0 562.7 jit_solution(7495215862793995918)
XLA Ops:
  15.4 106.9 %psum.15 = bf16[16,1024]{1,0:T(8,128)(2,1)S(1)} all-reduce(f32[16,1024]{1,0:T(8,128)S(1)} %pad_maximum_fusion), channel_id=1, replica_groups=mesh['grp'=16,'body'=32] {'body'}, use_global_device_ids=true, to_apply=%region_3.4 | all-reduce | flops 16384 | bytes 98304 | tf_op jit(solution)/shard_map/psum | solution.py:73
  122.4 40.8 %all-gather = bf16[256,32]{1,0:T(8,128)(2,1)S(1)} all-gather(bf16[16,32]{1,0:T(8,128)(2,1)S(1)} %pad_maximum_fusion.3), channel_id=2, replica_groups=mesh['grp'=16,'body'=32] {'grp'}, dimensions={0}, use_global_device_ids=true | all-gather | bytes 17408 | tf_op jit(solution)/shard_map/all_gather | solution.py:81
  167.9 41.5 %all-gather.2 = s32[32,1,32]{2,1,0:T(1,128)S(1)} all-gather(s32[1,1,32]{2,1,0:T(1,128)S(1)} %bitcast.161), channel_id=1, replica_groups=mesh['grp'=16,'body'=32] {'body'}, dimensions={0}, use_global_device_ids=true | all-gather | bytes 4224 | tf_op jit(solution)/shard_map/all_gather | solution.py:54
  211.7 118.9 %while.11 = (s32[]{:T(128)}, f32[8,4,16,512]{3,2,1,0:T(8,128)}, bf16[8,4,1,2,512]{4,3,1,2,0:T(2,128)(2,1)S(1)}, bf16[1,16,512]{2,1,0:T(8,128)(2,1)S(1)}, s32[]{:T(128)}) while((s32[]{:T(128)}, f32[8,4,16,512]{3,2,1,0:T(8,128)}, bf16[8,4,1,2,512]{4,3,1,2,0:T(2,128)(2,1)S(1)}, bf16[1,16,512]{2,1,0:T(8,128)(2,1)S(1)}, s32[]{:T(128)}) %tuple.28), condition=%wide.region_1.2_spmd, body=%wide.region_0.1_spmd.sunk | while | flops 33619968 | bytes 17474112 | solution.py:69
  211.9 2.8 tile.14
  214.7 4.4 slice.219
  219.1 6.1 %reshape.289 = bf16[4,1,2,256,511]{4,3,2,0,1:T(8,128)(2,1)S(1)} reshape(bf16[4,1,2,130816]{3,2,0,1:T(2,128)(2,1)} %slice.219) | data formatting | bytes 4186112 | tf_op jit(solution)/shard_map/while/body/eval_jaxpr/reshape | solution.py:32
  226.8 2.8 tile.14
  229.5 4.4 slice.219
  233.9 6.1 %reshape.289 = bf16[4,1,2,256,511]{4,3,2,0,1:T(8,128)(2,1)S(1)} reshape(bf16[4,1,2,130816]{3,2,0,1:T(2,128)(2,1)} %slice.219) | data formatting | bytes 4186112 | tf_op jit(solution)/shard_map/while/body/eval_jaxpr/reshape | solution.py:32
  244.4 4.4 slice.219
  248.8 6.1 %reshape.289 = bf16[4,1,2,256,511]{4,3,2,0,1:T(8,128)(2,1)S(1)} reshape(bf16[4,1,2,130816]{3,2,0,1:T(2,128)(2,1)} %slice.219) | data formatting | bytes 4186112 | tf_op jit(solution)/shard_map/while/body/eval_jaxpr/reshape | solution.py:32
  256.5 2.8 tile.14
  259.3 4.4 slice.219
  263.6 6.1 %reshape.289 = bf16[4,1,2,256,511]{4,3,2,0,1:T(8,128)(2,1)S(1)} reshape(bf16[4,1,2,130816]{3,2,0,1:T(2,128)(2,1)} %slice.219) | data formatting | bytes 4186112 | tf_op jit(solution)/shard_map/while/body/eval_jaxpr/reshape | solution.py:32
  274.1 4.4 slice.219
  278.5 6.1 %reshape.289 = bf16[4,1,2,256,511]{4,3,2,0,1:T(8,128)(2,1)S(1)} reshape(bf16[4,1,2,130816]{3,2,0,1:T(2,128)(2,1)} %slice.219) | data formatting | bytes 4186112 | tf_op jit(solution)/shard_map/while/body/eval_jaxpr/reshape | solution.py:32
  289.0 4.4 slice.219
  293.4 6.1 %reshape.289 = bf16[4,1,2,256,511]{4,3,2,0,1:T(8,128)(2,1)S(1)} reshape(bf16[4,1,2,130816]{3,2,0,1:T(2,128)(2,1)} %slice.219) | data formatting | bytes 4186112 | tf_op jit(solution)/shard_map/while/body/eval_jaxpr/reshape | solution.py:32
  303.8 4.4 slice.219
  308.2 6.1 %reshape.289 = bf16[4,1,2,256,511]{4,3,2,0,1:T(8,128)(2,1)S(1)} reshape(bf16[4,1,2,130816]{3,2,0,1:T(2,128)(2,1)} %slice.219) | data formatting | bytes 4186112 | tf_op jit(solution)/shard_map/while/body/eval_jaxpr/reshape | solution.py:32
  318.7 4.4 slice.219
  323.1 6.1 %reshape.289 = bf16[4,1,2,256,511]{4,3,2,0,1:T(8,128)(2,1)S(1)} reshape(bf16[4,1,2,130816]{3,2,0,1:T(2,128)(2,1)} %slice.219) | data formatting | bytes 4186112 | tf_op jit(solution)/shard_map/while/body/eval_jaxpr/reshape | solution.py:32
  333.0 221.5 %all-reduce.2.cloned.1.call-done = f32[32,16,512]{2,1,0:T(8,128)} async-done(((f32[32,16,512]{2,1,0:T(8,128)}), f32[32,16,512]{2,1,0:T(8,128)}) %all-reduce.2.cloned.1.call-update) | async-done | bytes 1048592 | tf_op jit(solution)/shard_map/psum | solution.py:70
  (112 shorter events, 44.1 us)
Async XLA Ops:
  6.5 204.3 %copy-start = (bf16[225,2,512]{2,1,0:T(2,128)(2,1)S(1)}, bf16[225,2,512]{2,1,0:T(2,128)(2,1)}, u32[]{:S(2)}) copy-start(bf16[225,2,512]{2,1,0:T(2,128)(2,1)} %param.14) | copy-start | bytes 1382404
  6.5 156.6 %copy-start.2 = (bf16[1,16,2,16,512]{4,3,2,1,0:T(8,128)(2,1)S(1)}, bf16[1,16,2,16,512]{4,3,2,1,0:T(8,128)(2,1)}, u32[]{:S(2)}) copy-start(bf16[1,16,2,16,512]{4,3,2,1,0:T(8,128)(2,1)} %param.19) | copy-start | bytes 1572868
  6.5 324.1 %all-gather.5.cloned.1.call-start = ((), (), s32[]{:S(2)}) async-start(), calls=%async_computation.1 | async-start | bytes 2162688 | tf_op jit(solution)/shard_map/all_gather | solution.py:9
  13.1 152.1 %copy-start.5 = (s32[32]{0:T(128)S(1)}, s32[32]{0:T(128)}, u32[]{:S(2)}) copy-start(s32[32]{0:T(128)} %param.16) | copy-start | bytes 388
  13.1 154.8 %copy-start.4 = (s32[1,32]{1,0:T(1,128)S(1)}, s32[1,32]{1,0:T(1,128)}, u32[]{:S(2)}) copy-start(s32[1,32]{1,0:T(1,128)} %param.15) | copy-start | bytes 388
  165.1 389.4 %all-reduce.2.cloned.1.call-start = ((), (), s32[]{:S(2)}) async-start(), calls=%async_computation | async-start | bytes 2097152 | tf_op jit(solution)/shard_map/psum | solution.py:70
  330.6 1.8 copy-start.1
  330.6 223.9 %copy-start.3 = (f32[1,16,512]{2,1,0:T(8,128)S(1)}, f32[1,16,512]{2,1,0:T(8,128)}, u32[]{:S(2)}) copy-start(f32[1,16,512]{2,1,0:T(8,128)} %param.12) | copy-start | bytes 98308
Sparse Core Ops, SparseCore 0:
  165.2 69.3 all-gather.4
  330.7 223.7 all-reduce.1
